TPU v7x, 1024 devices: a whole 4x8x16 slice. The times are simulated.
1024 devices in a mesh: blk: 32 (over z_lo, x), group: 32 (over z_hi, y, core).
Axes of the slice: x: 4, y: 8, z: 16 (z_hi: 2, z_lo: 8; z = z_hi * 8 + z_lo), core: 2. Of those that a mesh axis runs over, the one named last changes fastest.
Arguments:
- user_factors: float32 [262144, 256], P(('blk', 'group')), may hold values from -1.5 to 1.5
- user_state: float32 [262144, 256], P(('blk', 'group')), may hold values from 0.5 to 20
- item_factors: float32 [262144, 256], P(('blk', 'group')), may hold values from -1.5 to 1.5
- item_state: float32 [262144, 256], P(('blk', 'group')), may hold values from 0.5 to 20
- counts: int32 [262144, 1024], P(('blk', 'group')), may hold values from 0 to 5
Outputs:
- users_out: float32 [262144, 256], P(('blk', 'group'))
- user_state_out: float32 [262144, 256], P(('blk', 'group'))
- items_out: float32 [262144, 256], P(('blk', 'group'))
- item_state_out: float32 [262144, 256], P(('blk', 'group'))
All inputs are finite; a program needn't handle non-finite values.
Results may differ from a plain program's by a relative error of at most 0.0003.
Values sent between devices are 32-bit elements; how exact they have to be, the bound alone decides.
A program may use at most 32 MiB of HBM per device.

v0:
```python
import jax
import jax.numpy as jnp
from jax import lax
from jax.sharding import PartitionSpec as P

STRATA = 4


conf_scale = 0.5
ridge_weight = 0.01
step_rate = 0.1


def passed_along(value, axis, steps):
    count = lax.axis_size(axis)
    pairs = [(source, (source + steps) % count) for source in range(count)]
    return lax.ppermute(value, axis, pairs)


def transposed_dot(left, right):
    return lax.dot_general(left, right, (((0,), (0,)), ((), ())), precision=lax.Precision.HIGHEST)


def item_update(weighted_gap, users, items, item_acc):
    item_grad = 2.0 * transposed_dot(weighted_gap, users) + 2.0 * ridge_weight * items
    item_acc = item_acc + item_grad * item_grad
    return (items - step_rate * item_grad / jnp.sqrt(item_acc), item_acc)


def body(user_factors, user_state, item_factors, item_state, counts):
    highest = lax.Precision.HIGHEST
    item_rows = item_factors.shape[0]
    users, user_acc = (user_factors, user_state)
    items, item_acc = (item_factors, item_state)
    for stratum in range(STRATA):
        count_tile = counts[:, stratum * item_rows : (stratum + 1) * item_rows]
        predicted = lax.dot_general(users, items, (((1,), (1,)), ((), ())), precision=highest)
        prefer = (count_tile > 0).astype(jnp.float32)
        confidence = 1.0 + conf_scale * count_tile.astype(jnp.float32)
        weighted_gap = confidence * (predicted - prefer)
        user_grad = (
            2.0 * jnp.dot(weighted_gap, items, precision=highest) + 2.0 * ridge_weight * users
        )
        next_items, next_acc = item_update(weighted_gap, users, items, item_acc)
        next_items, next_acc = passed_along((next_items, next_acc), "blk", 1)
        user_acc = user_acc + user_grad * user_grad
        users = users - step_rate * user_grad / jnp.sqrt(user_acc)
        items, item_acc = (next_items, next_acc)
    items, item_acc = passed_along((items, item_acc), "group", 1)
    return (users, user_acc, items, item_acc)


def solution(mesh):
    return jax.shard_map(
        body,
        mesh=mesh,
        in_specs=(
            P(("blk", "group"), None),
            P(("blk", "group"), None),
            P(("blk", "group"), None),
            P(("blk", "group"), None),
            P(("blk", "group"), None),
        ),
        out_specs=(
            P(("blk", "group"), None),
            P(("blk", "group"), None),
            P(("blk", "group"), None),
            P(("blk", "group"), None),
        ),
        check_vma=False,
    )
```

profile of v0, /device:TPU:56, one launch (start us, length us, event | category | flops | bytes accessed | tf_op | source)
XLA Modules:
  0.0 129.2 jit_solution(1431657815803136892)
XLA Ops:
  0.7 1.6 %fusion.8 = f32[256,256]{1,0:T(8,128)S(1)} fusion(f32[256,256]{1,0:T(8,128)} %param.5, f32[256,256]{1,0:T(8,128)} %param.7, s32[256,1024]{1,0:T(8,128)} %param.9), kind=kOutput, calls=%fused_computation.20 | convolution fusion | flops 201785344 | bytes 1048576 | tf_op jit(solution)/shard_map/dot_general | solution.py:37
  2.3 0.6 multiply_subtract_fusion.6
  2.9 3.5 %collective-permute-start = (f32[256,256]{1,0:T(8,128)S(1)}, f32[256,256]{1,0:T(8,128)S(1)}, u32[]{:S(2)}, u32[]{:S(2)}) collective-permute-start(f32[256,256]{1,0:T(8,128)S(1)} %get-tuple-element.8), channel_id=1, source_target_pairs={{0,32},{32,64},{64,96},{96,128},{128,160},{160,192},{192,224},{224... | collective-permute-start | bytes 786440 | tf_op jit(solution)/shard_map/ppermute | solution.py:17
  6.5 3.4 %collective-permute-start.1 = (f32[256,256]{1,0:T(8,128)S(1)}, f32[256,256]{1,0:T(8,128)S(1)}, u32[]{:S(2)}, u32[]{:S(2)}) collective-permute-start(f32[256,256]{1,0:T(8,128)S(1)} %get-tuple-element.9), channel_id=1, source_target_pairs={{0,32},{32,64},{64,96},{96,128},{128,160},{160,192},{192,224},{224... | collective-permute-start | bytes 786440 | tf_op jit(solution)/shard_map/ppermute | solution.py:17
  9.9 0.4 multiply_subtract_fusion.7
  10.3 18.4 %collective-permute-done = f32[256,256]{1,0:T(8,128)S(1)} collective-permute-done((f32[256,256]{1,0:T(8,128)S(1)}, f32[256,256]{1,0:T(8,128)S(1)}, u32[]{:S(2)}, u32[]{:S(2)}) %collective-permute-start) | collective-permute-done | bytes 262176 | tf_op jit(solution)/shard_map/ppermute | solution.py:17
  28.7 0.4 fusion.5
  29.2 4.4 %collective-permute-done.1 = f32[256,256]{1,0:T(8,128)S(1)} collective-permute-done((f32[256,256]{1,0:T(8,128)S(1)}, f32[256,256]{1,0:T(8,128)S(1)}, u32[]{:S(2)}, u32[]{:S(2)}) %collective-permute-start.1) | collective-permute-done | bytes 262176 | tf_op jit(solution)/shard_map/ppermute | solution.py:17
  33.5 0.6 multiply_add_fusion.6
  34.1 1.9 %collective-permute-start.3 = (f32[256,256]{1,0:T(8,128)S(1)}, f32[256,256]{1,0:T(8,128)S(1)}, u32[]{:S(2)}, u32[]{:S(2)}) collective-permute-start(f32[256,256]{1,0:T(8,128)S(1)} %get-tuple-element.14), channel_id=1, source_target_pairs={{0,32},{32,64},{64,96},{96,128},{128,160},{160,192},{192,224},{224... | collective-permute-start | bytes 786440 | tf_op jit(solution)/shard_map/ppermute | solution.py:17
  36.1 1.9 %collective-permute-start.2 = (f32[256,256]{1,0:T(8,128)S(1)}, f32[256,256]{1,0:T(8,128)S(1)}, u32[]{:S(2)}, u32[]{:S(2)}) collective-permute-start(f32[256,256]{1,0:T(8,128)S(1)} %get-tuple-element.15), channel_id=1, source_target_pairs={{0,32},{32,64},{64,96},{96,128},{128,160},{160,192},{192,224},{224... | collective-permute-start | bytes 786440 | tf_op jit(solution)/shard_map/ppermute | solution.py:17
  38.0 0.4 multiply_subtract_fusion.5
  38.5 19.4 %collective-permute-done.2 = f32[256,256]{1,0:T(8,128)S(1)} collective-permute-done((f32[256,256]{1,0:T(8,128)S(1)}, f32[256,256]{1,0:T(8,128)S(1)}, u32[]{:S(2)}, u32[]{:S(2)}) %collective-permute-start.2) | collective-permute-done | bytes 262176 | tf_op jit(solution)/shard_map/ppermute | solution.py:17
  57.9 0.4 fusion.3
  58.3 0.6 convolution_multiply_fusion.2
  58.9 0.1 multiply_add_fusion.3
  59.0 1.9 %collective-permute-start.5 = (f32[256,256]{1,0:T(8,128)S(1)}, f32[256,256]{1,0:T(8,128)S(1)}, u32[]{:S(2)}, u32[]{:S(2)}) collective-permute-start(f32[256,256]{1,0:T(8,128)S(1)} %get-tuple-element.12), channel_id=1, source_target_pairs={{0,32},{32,64},{64,96},{96,128},{128,160},{160,192},{192,224},{224... | collective-permute-start | bytes 786440 | tf_op jit(solution)/shard_map/ppermute | solution.py:17
  60.9 1.9 %collective-permute-start.4 = (f32[256,256]{1,0:T(8,128)S(1)}, f32[256,256]{1,0:T(8,128)S(1)}, u32[]{:S(2)}, u32[]{:S(2)}) collective-permute-start(f32[256,256]{1,0:T(8,128)S(1)} %get-tuple-element.13), channel_id=1, source_target_pairs={{0,32},{32,64},{64,96},{96,128},{128,160},{160,192},{192,224},{224... | collective-permute-start | bytes 786440 | tf_op jit(solution)/shard_map/ppermute | solution.py:17
  62.8 0.4 multiply_subtract_fusion.3
  63.3 18.5 %collective-permute-done.4 = f32[256,256]{1,0:T(8,128)S(1)} collective-permute-done((f32[256,256]{1,0:T(8,128)S(1)}, f32[256,256]{1,0:T(8,128)S(1)}, u32[]{:S(2)}, u32[]{:S(2)}) %collective-permute-start.4) | collective-permute-done | bytes 262176 | tf_op jit(solution)/shard_map/ppermute | solution.py:17
  81.8 0.4 fusion.1
  82.2 0.6 convolution_multiply_fusion
  82.9 1.9 %collective-permute-start.8 = (f32[256,256]{1,0:T(8,128)S(1)}, f32[256,256]{1,0:T(8,128)S(1)}, u32[]{:S(2)}, u32[]{:S(2)}) collective-permute-start(f32[256,256]{1,0:T(8,128)S(1)} %get-tuple-element.10), channel_id=1, source_target_pairs={{0,32},{32,64},{64,96},{96,128},{128,160},{160,192},{192,224},{224... | collective-permute-start | bytes 786440 | tf_op jit(solution)/shard_map/ppermute | solution.py:17
  84.8 1.9 %collective-permute-start.6 = (f32[256,256]{1,0:T(8,128)S(1)}, f32[256,256]{1,0:T(8,128)S(1)}, u32[]{:S(2)}, u32[]{:S(2)}) collective-permute-start(f32[256,256]{1,0:T(8,128)S(1)} %get-tuple-element.11), channel_id=1, source_target_pairs={{0,32},{32,64},{64,96},{96,128},{128,160},{160,192},{192,224},{224... | collective-permute-start | bytes 786440 | tf_op jit(solution)/shard_map/ppermute | solution.py:17
  86.8 27.8 %collective-permute-done.8 = f32[256,256]{1,0:T(8,128)S(1)} collective-permute-done((f32[256,256]{1,0:T(8,128)S(1)}, f32[256,256]{1,0:T(8,128)S(1)}, u32[]{:S(2)}, u32[]{:S(2)}) %collective-permute-start.8) | collective-permute-done | bytes 262176 | tf_op jit(solution)/shard_map/ppermute | solution.py:17
  114.5 1.9 %collective-permute-start.9 = (f32[256,256]{1,0:T(8,128)S(1)}, f32[256,256]{1,0:T(8,128)S(1)}, u32[]{:S(2)}, u32[]{:S(2)}) collective-permute-start(f32[256,256]{1,0:T(8,128)S(1)} %collective-permute-done.8), channel_id=1, source_target_pairs={{0,1},{1,2},{2,3},{3,4},{4,5},{5,6},{6,7},{7,8},{8,9},{9,10},{10,1... | collective-permute-start | bytes 786440 | tf_op jit(solution)/shard_map/ppermute | solution.py:17
  116.4 3.7 %collective-permute-done.6 = f32[256,256]{1,0:T(8,128)S(1)} collective-permute-done((f32[256,256]{1,0:T(8,128)S(1)}, f32[256,256]{1,0:T(8,128)S(1)}, u32[]{:S(2)}, u32[]{:S(2)}) %collective-permute-start.6) | collective-permute-done | bytes 262176 | tf_op jit(solution)/shard_map/ppermute | solution.py:17
  120.1 1.9 %collective-permute-start.7 = (f32[256,256]{1,0:T(8,128)S(1)}, f32[256,256]{1,0:T(8,128)S(1)}, u32[]{:S(2)}, u32[]{:S(2)}) collective-permute-start(f32[256,256]{1,0:T(8,128)S(1)} %collective-permute-done.6), channel_id=1, source_target_pairs={{0,1},{1,2},{2,3},{3,4},{4,5},{5,6},{6,7},{7,8},{8,9},{9,10},{10,1... | collective-permute-start | bytes 786440 | tf_op jit(solution)/shard_map/ppermute | solution.py:17
  122.1 1.2 multiply_subtract_fusion.1
  123.3 4.5 %collective-permute-done.7 = f32[256,256]{1,0:T(8,128)S(1)} collective-permute-done((f32[256,256]{1,0:T(8,128)S(1)}, f32[256,256]{1,0:T(8,128)S(1)}, u32[]{:S(2)}, u32[]{:S(2)}) %collective-permute-start.7) | collective-permute-done | bytes 262176 | tf_op jit(solution)/shard_map/ppermute | solution.py:17
  127.8 0.7 copy.11
  128.5 0.7 copy.12
  (14 shorter events, 0.1 us)
Async XLA Ops:
  0.6 1.6 %copy-start.1 = (f32[256,256]{1,0:T(8,128)S(1)}, f32[256,256]{1,0:T(8,128)}, u32[]{:S(2)}) copy-start(f32[256,256]{1,0:T(8,128)} %param.7) | copy-start | bytes 786436
  0.6 1.6 %copy-start = (f32[256,256]{1,0:T(8,128)S(1)}, f32[256,256]{1,0:T(8,128)}, u32[]{:S(2)}) copy-start(f32[256,256]{1,0:T(8,128)} %param.5) | copy-start | bytes 786436
  0.7 1.6 %copy-start.4 = (f32[256,256]{1,0:T(8,128)S(1)}, f32[256,256]{1,0:T(8,128)}, u32[]{:S(2)}) copy-start(f32[256,256]{1,0:T(8,128)} %param.8) | copy-start | bytes 786436
  2.3 7.6 %copy-start.2 = (f32[256,256]{1,0:T(8,128)S(1)}, f32[256,256]{1,0:T(8,128)}, u32[]{:S(2)}) copy-start(f32[256,256]{1,0:T(8,128)} %param.6) | copy-start | bytes 786436
  2.9 25.8 %copy-start.3 = (s32[256,1024]{1,0:T(8,128)S(1)}, s32[256,1024]{1,0:T(8,128)}, u32[]{:S(2)}) copy-start(s32[256,1024]{1,0:T(8,128)} %param.9) | copy-start | bytes 3145732
  2.9 25.8 %collective-permute-start = (f32[256,256]{1,0:T(8,128)S(1)}, f32[256,256]{1,0:T(8,128)S(1)}, u32[]{:S(2)}, u32[]{:S(2)}) collective-permute-start(f32[256,256]{1,0:T(8,128)S(1)} %get-tuple-element.8), channel_id=1, source_target_pairs={{0,32},{32,64},{64,96},{96,128},{128,160},{160,192},{192,224},{224... | collective-permute-start | bytes 786440 | tf_op jit(solution)/shard_map/ppermute | solution.py:17
  6.5 27.0 %collective-permute-start.1 = (f32[256,256]{1,0:T(8,128)S(1)}, f32[256,256]{1,0:T(8,128)S(1)}, u32[]{:S(2)}, u32[]{:S(2)}) collective-permute-start(f32[256,256]{1,0:T(8,128)S(1)} %get-tuple-element.9), channel_id=1, source_target_pairs={{0,32},{32,64},{64,96},{96,128},{128,160},{160,192},{192,224},{224... | collective-permute-start | bytes 786440 | tf_op jit(solution)/shard_map/ppermute | solution.py:17
  34.1 24.8 %collective-permute-start.3 = (f32[256,256]{1,0:T(8,128)S(1)}, f32[256,256]{1,0:T(8,128)S(1)}, u32[]{:S(2)}, u32[]{:S(2)}) collective-permute-start(f32[256,256]{1,0:T(8,128)S(1)} %get-tuple-element.14), channel_id=1, source_target_pairs={{0,32},{32,64},{64,96},{96,128},{128,160},{160,192},{192,224},{224... | collective-permute-start | bytes 786440 | tf_op jit(solution)/shard_map/ppermute | solution.py:17
  36.1 21.8 %collective-permute-start.2 = (f32[256,256]{1,0:T(8,128)S(1)}, f32[256,256]{1,0:T(8,128)S(1)}, u32[]{:S(2)}, u32[]{:S(2)}) collective-permute-start(f32[256,256]{1,0:T(8,128)S(1)} %get-tuple-element.15), channel_id=1, source_target_pairs={{0,32},{32,64},{64,96},{96,128},{128,160},{160,192},{192,224},{224... | collective-permute-start | bytes 786440 | tf_op jit(solution)/shard_map/ppermute | solution.py:17
  59.0 23.8 %collective-permute-start.5 = (f32[256,256]{1,0:T(8,128)S(1)}, f32[256,256]{1,0:T(8,128)S(1)}, u32[]{:S(2)}, u32[]{:S(2)}) collective-permute-start(f32[256,256]{1,0:T(8,128)S(1)} %get-tuple-element.12), channel_id=1, source_target_pairs={{0,32},{32,64},{64,96},{96,128},{128,160},{160,192},{192,224},{224... | collective-permute-start | bytes 786440 | tf_op jit(solution)/shard_map/ppermute | solution.py:17
  60.9 20.9 %collective-permute-start.4 = (f32[256,256]{1,0:T(8,128)S(1)}, f32[256,256]{1,0:T(8,128)S(1)}, u32[]{:S(2)}, u32[]{:S(2)}) collective-permute-start(f32[256,256]{1,0:T(8,128)S(1)} %get-tuple-element.13), channel_id=1, source_target_pairs={{0,32},{32,64},{64,96},{96,128},{128,160},{160,192},{192,224},{224... | collective-permute-start | bytes 786440 | tf_op jit(solution)/shard_map/ppermute | solution.py:17
  82.9 31.6 %collective-permute-start.8 = (f32[256,256]{1,0:T(8,128)S(1)}, f32[256,256]{1,0:T(8,128)S(1)}, u32[]{:S(2)}, u32[]{:S(2)}) collective-permute-start(f32[256,256]{1,0:T(8,128)S(1)} %get-tuple-element.10), channel_id=1, source_target_pairs={{0,32},{32,64},{64,96},{96,128},{128,160},{160,192},{192,224},{224... | collective-permute-start | bytes 786440 | tf_op jit(solution)/shard_map/ppermute | solution.py:17
  84.8 35.3 %collective-permute-start.6 = (f32[256,256]{1,0:T(8,128)S(1)}, f32[256,256]{1,0:T(8,128)S(1)}, u32[]{:S(2)}, u32[]{:S(2)}) collective-permute-start(f32[256,256]{1,0:T(8,128)S(1)} %get-tuple-element.11), channel_id=1, source_target_pairs={{0,32},{32,64},{64,96},{96,128},{128,160},{160,192},{192,224},{224... | collective-permute-start | bytes 786440 | tf_op jit(solution)/shard_map/ppermute | solution.py:17
  114.5 8.8 %collective-permute-start.9 = (f32[256,256]{1,0:T(8,128)S(1)}, f32[256,256]{1,0:T(8,128)S(1)}, u32[]{:S(2)}, u32[]{:S(2)}) collective-permute-start(f32[256,256]{1,0:T(8,128)S(1)} %collective-permute-done.8), channel_id=1, source_target_pairs={{0,1},{1,2},{2,3},{3,4},{4,5},{5,6},{6,7},{7,8},{8,9},{9,10},{10,1... | collective-permute-start | bytes 786440 | tf_op jit(solution)/shard_map/ppermute | solution.py:17
  120.1 7.7 %collective-permute-start.7 = (f32[256,256]{1,0:T(8,128)S(1)}, f32[256,256]{1,0:T(8,128)S(1)}, u32[]{:S(2)}, u32[]{:S(2)}) collective-permute-start(f32[256,256]{1,0:T(8,128)S(1)} %collective-permute-done.6), channel_id=1, source_target_pairs={{0,1},{1,2},{2,3},{3,4},{4,5},{5,6},{6,7},{7,8},{8,9},{9,10},{10,1... | collective-permute-start | bytes 786440 | tf_op jit(solution)/shard_map/ppermute | solution.py:17
where the time goes:
time: 130 us; the launch traced here: 129 us
  waiting for transfers between devices  96.7 us (74%)
  starting transfers between devices  22.3 us (17%)
  matrix products  7.81 us (6%)
  local copies, waits for them, and re-layouts  1.43 us (1%)
    ppermute x10, waiting for transfers between devices, passed_along(): return lax.ppermute(value, axis, pairs)  96.7 us
    ppermute x10, starting transfers between devices, passed_along(): return lax.ppermute(value, axis, pairs)  22.3 us
    dot_general x4, matrix products, body(): lax.dot_general(users, items, (((1,), (1,)), ((), ())), precision=highest)  2.84 us
  transfers between devices with their start and end apart: 10, of which 7 were waited for; matrix products, arithmetic and copies ran while one was open for 4% of the time, Pallas kernels for 0%

commit v1 on v0

v1 whole, which is shorter than its diff:
```python
import functools
import jax
import jax.numpy as jnp
from jax import lax
from jax.experimental import pallas as pl
from jax.experimental.pallas import tpu as pltpu
from jax.sharding import PartitionSpec as P

STRATA = 4
R = 256
XS = 4
NC = 4
CH = R // NC
MESH = pl.DeviceIdType.MESH

conf_scale = 0.5
ridge_weight = 0.01
step_rate = 0.1

NT = (((1,), (1,)), ((), ()))
NN = (((1,), (0,)), ((), ()))
TN = (((0,), (0,)), ((), ()))


def split(value):
    high = value.astype(jnp.bfloat16)
    return high, (value - high.astype(jnp.float32)).astype(jnp.bfloat16)


def dot3(left, right, dims):
    (lh, ll), (rh, rl) = left, right
    dot = functools.partial(lax.dot_general, dimension_numbers=dims, preferred_element_type=jnp.float32)
    return dot(lh, rh) + (dot(lh, rl) + dot(ll, rh))


def weigh(counts, predicted):
    prefer = (counts > 0).astype(jnp.float32)
    return (1.0 + conf_scale * counts) * (predicted - prefer)


def adagrad(value, acc, grad):
    acc = acc + grad * grad
    return value - step_rate * grad * lax.rsqrt(acc), acc


def kernel(n_blk, n_group, u_in, a_in, v_in, b_in, k_in, u_out, a_out, v_out, b_out,
           users, user_acc, home_v, home_b, kraw, kt, vin, gin, gout, uh, ul, vh, vl, gh, gl,
           load, store, vsend, vrecv, gsend, grecv, msend, mrecv, fsend, frecv):
    b, g = lax.axis_index("blk"), lax.axis_index("group")
    x = lax.rem(b, XS)
    plane = b - x

    def at(blk, group=g):
        return {"blk": blk, "group": group}

    def ring(steps):
        return at(plane + lax.rem(x + steps, XS))

    nxt, prv = lax.rem(b + XS, n_blk), lax.rem(b + n_blk - XS, n_blk)
    final = at(jnp.where(x == 0, nxt, b), lax.rem(g + 1, n_group))
    final_from = at(jnp.where(x == 0, prv, b), lax.rem(g + n_group - 1, n_group))

    loads = [
        pltpu.make_async_copy(u_in, users, load.at[0]),
        pltpu.make_async_copy(v_in, home_v.at[0], load.at[1]),
        pltpu.make_async_copy(k_in, kraw, load.at[2]),
        pltpu.make_async_copy(b_in, home_b.at[0], load.at[3]),
        pltpu.make_async_copy(a_in, user_acc, load.at[4]),
    ]
    for copy in loads:
        copy.start()
    barrier = pltpu.get_barrier_semaphore()
    for device in (ring(1), ring(2), ring(3), at(nxt), at(prv), final, final_from):
        pl.semaphore_signal(barrier, inc=1, device_id=device, device_id_type=MESH)

    def rows(k):
        return pl.ds(k * CH, CH)

    def slot(s):
        return (x >= XS - s).astype(jnp.int32)

    def v_copy(s, k):
        return pltpu.make_async_remote_copy(
            home_v.at[slot(s), rows(k)], vin.at[s - 1, rows(k)], vsend.at[s - 1, k], vrecv.at[s - 1, k],
            device_id=ring(s), device_id_type=MESH)

    def g_copy(s, k):
        return pltpu.make_async_remote_copy(
            gout.at[s - 1, rows(k)], gin.at[s - 1, rows(k)], gsend.at[s - 1, k], grecv.at[s - 1, k],
            device_id=ring(XS - s), device_id_type=MESH)

    def m_copy(which, k):
        ref = (home_v, home_b)[which]
        return pltpu.make_async_remote_copy(
            ref.at[0, rows(k)], ref.at[1, rows(k)], msend.at[which, k], mrecv.at[which, k],
            device_id=at(nxt), device_id_type=MESH)

    def f_copy(which, k):
        ref, out = ((home_v, v_out), (home_b, b_out))[which]
        return pltpu.make_async_remote_copy(
            ref.at[slot(3), rows(k)], out.at[rows(k)], fsend.at[which, k], frecv.at[which, k],
            device_id=final, device_id_type=MESH)

    def send_v(s, k):
        @pl.when(x == XS - s)
        def _():
            m_copy(0, k).start()

        @pl.when(x != XS - s)
        def _():
            v_copy(s, k).start()

    def send_b(s):
        @pl.when(x == XS - s)
        def _():
            for k in range(NC):
                m_copy(1, k).start()

    def update_users(grad):
        grad = 2.0 * grad + (2.0 * ridge_weight) * users[...]
        users[...], user_acc[...] = adagrad(users[...], user_acc[...], grad)
        uh[...], ul[...] = split(users[...])

    loads[0].wait()
    uh[...], ul[...] = split(users[...])
    loads[1].wait()
    vh[...], vl[...] = split(home_v[0])
    loads[2].wait()
    usplit, vsplit = (uh[...], ul[...]), (vh[...], vl[...])
    gap = split(weigh(kraw[:, :R].astype(jnp.float32), dot3(usplit, vsplit, NT)))
    grad = 2.0 * dot3(gap, usplit, TN) + (2.0 * ridge_weight) * home_v[0]
    loads[3].wait()
    home_v[0], home_b[0] = adagrad(home_v[0], home_b[0], grad)
    pl.semaphore_wait(barrier, 7)
    for k in range(NC):
        send_v(1, k)
    send_b(1)
    loads[4].wait()
    update_users(dot3(gap, vsplit, NN))
    for s in range(1, STRATA):
        kt[s - 1] = kraw[:, s * R : (s + 1) * R].astype(jnp.float32).T

    for s in range(1, STRATA):
        for k in range(NC):
            @pl.when(x == XS - s)
            def _():
                m_copy(0, k).wait_recv()
                v_copy(s, k).start()

            v_copy(s, k).wait_recv()
            items = vin[s - 1, rows(k)]
            items_split = split(items)
            vh[rows(k)], vl[rows(k)] = items_split
            usplit = (uh[...], ul[...])
            gap = split(weigh(kt[s - 1, rows(k)], dot3(items_split, usplit, NT)))
            gh[rows(k)], gl[rows(k)] = gap
            gout[s - 1, rows(k)] = 2.0 * dot3(gap, usplit, NN) + (2.0 * ridge_weight) * items
            g_copy(s, k).start()
        update_users(dot3((gh[...], gl[...]), (vh[...], vl[...]), TN))
        if s == STRATA - 1:
            stores = [pltpu.make_async_copy(users, u_out, store.at[0]), pltpu.make_async_copy(user_acc, a_out, store.at[1])]
            for copy in stores:
                copy.start()
        for k in range(NC):
            @pl.when(x == XS - s)
            def _():
                m_copy(1, k).wait_recv()

            v_copy(s, k).wait_send()
            g_copy(s, k).wait_recv()
            now = slot(s)
            home_v[now, rows(k)], home_b[now, rows(k)] = adagrad(home_v[now, rows(k)], home_b[now, rows(k)], gin[s - 1, rows(k)])
            if s < STRATA - 1:
                send_v(s + 1, k)
            else:
                f_copy(0, k).start()
                f_copy(1, k).start()
        if s < STRATA - 1:
            send_b(s + 1)

    for s in range(1, STRATA):
        for k in range(NC):
            g_copy(s, k).wait_send()

    @pl.when(x != 0)
    def _():
        for which in range(2):
            for k in range(NC):
                m_copy(which, k).wait_send()

    for which in range(2):
        for k in range(NC):
            f_copy(which, k).wait()
    for copy in stores:
        copy.wait()


def body(user_factors, user_state, item_factors, item_state, counts):
    anywhere = pl.BlockSpec(memory_space=pl.ANY)
    block = jax.ShapeDtypeStruct((R, R), jnp.float32)
    f32, bf16 = jnp.float32, jnp.bfloat16
    dma = pltpu.SemaphoreType.DMA
    return pl.pallas_call(
        functools.partial(kernel, lax.axis_size("blk"), lax.axis_size("group")),
        out_shape=(block,) * 4,
        in_specs=[anywhere] * 5,
        out_specs=(anywhere,) * 4,
        scratch_shapes=[
            pltpu.VMEM((R, R), f32), pltpu.VMEM((R, R), f32),
            pltpu.VMEM((2, R, R), f32), pltpu.VMEM((2, R, R), f32),
            pltpu.VMEM((R, STRATA * R), jnp.int32), pltpu.VMEM((3, R, R), f32),
            pltpu.VMEM((3, R, R), f32), pltpu.VMEM((3, R, R), f32), pltpu.VMEM((3, R, R), f32),
            pltpu.VMEM((R, R), bf16), pltpu.VMEM((R, R), bf16),
            pltpu.VMEM((R, R), bf16), pltpu.VMEM((R, R), bf16),
            pltpu.VMEM((R, R), bf16), pltpu.VMEM((R, R), bf16),
            dma((5,)), dma((2,)),
            dma((3, NC)), dma((3, NC)), dma((3, NC)), dma((3, NC)),
            dma((2, NC)), dma((2, NC)), dma((2, NC)), dma((2, NC)),
        ],
        compiler_params=pltpu.CompilerParams(collective_id=0, has_side_effects=True, vmem_limit_bytes=32 * 2**20),
        name="strata",
    )(user_factors, user_state, item_factors, item_state, counts)


def solution(mesh):
    spec = P(("blk", "group"), None)
    return jax.shard_map(body, mesh=mesh, in_specs=(spec,) * 5, out_specs=(spec,) * 4, check_vma=False)
```

time: 130 us -> 115 us (0.88)
  the two profiles are of different devices: /device:TPU:56 before, /device:TPU:128 now
where the time goes in v1:
time: 115 us; the launch traced here: 114 us
  Pallas kernels  106 us (92%)
  local copies, waits for them, and re-layouts  7.83 us (7%)
    pallas_call x1, Pallas kernels, body(): pl.pallas_call(functools.partial(kernel, lax.axis_size('blk'), lax.axis_s...  106 us
    unnamed x14, local copies, waits for them, and re-layouts  7.83 us

profile of v1, /device:TPU:128, one launch (start us, length us, event | category | flops | bytes accessed | tf_op | source)
XLA Modules:
  0.0 114.4 jit_solution(8039331123573423053)
XLA Ops:
  0.6 0.0 copy-start
  0.6 1.2 %copy-done = s32[256,1024]{1,0:T(8,128)S(1)} copy-done((s32[256,1024]{1,0:T(8,128)S(1)}, s32[256,1024]{1,0:T(8,128)}, u32[]{:S(2)}) %copy-start) | copy-done | bytes 1048600
  1.9 0.0 copy-start.1
  1.9 0.9 copy-done.1
  2.8 0.0 copy-start.2
  2.8 0.9 copy-done.2
  3.8 0.0 copy-start.3
  3.8 0.9 copy-done.3
  4.7 0.0 copy-start.4
  4.7 0.9 copy-done.4
  5.7 105.9 %strata.1 = (f32[256,256]{1,0:T(8,128)S(1)}, f32[256,256]{1,0:T(8,128)S(1)}, f32[256,256]{1,0:T(8,128)S(1)}, f32[256,256]{1,0:T(8,128)S(1)}) custom-call(f32[256,256]{1,0:T(8,128)S(1)} %copy-done.1, f32[256,256]{1,0:T(8,128)S(1)} %copy-done.2, f32[256,256]{1,0:T(8,128)S(1)} %copy-done.3, f32[256,256]{1,0:T(8,128)S(1)} %copy-done.4, s32[256,1024]{1,0:T(8,128)S(1)} %copy-done), custom_call_target="tpu_custom_call" | custom-call | tf_op jit(solution)/shard_map/strata/pallas_call | solution.py:203
  111.6 0.7 copy.13
  112.3 0.7 copy.14
  113.0 0.7 copy.15
  113.7 0.7 copy.16
Async XLA Ops:
  0.6 1.2 %copy-start = (s32[256,1024]{1,0:T(8,128)S(1)}, s32[256,1024]{1,0:T(8,128)}, u32[]{:S(2)}) copy-start(s32[256,1024]{1,0:T(8,128)} %k_in.1) | copy-start | bytes 3145732
  1.9 0.9 copy-start.1
  2.8 0.9 copy-start.2
  3.8 0.9 copy-start.3
  4.7 0.9 copy-start.4

commit v2 on v1

--- a/solution.py
+++ b/solution.py
@@ -9,8 +9,10 @@
 STRATA = 4
 R = 256
 XS = 4
+YC = 16
 NC = 4
 CH = R // NC
+HALF = NC // 2
 MESH = pl.DeviceIdType.MESH
 
 conf_scale = 0.5
@@ -45,7 +47,7 @@
 
 def kernel(n_blk, n_group, u_in, a_in, v_in, b_in, k_in, u_out, a_out, v_out, b_out,
            users, user_acc, home_v, home_b, kraw, kt, vin, gin, gout, uh, ul, vh, vl, gh, gl,
-           load, store, vsend, vrecv, gsend, grecv, msend, mrecv, fsend, frecv):
+           relay, load, store, vsend, vrecv, gsend, grecv, msend, mrecv, fsend, frecv, lsend, lrecv):
     b, g = lax.axis_index("blk"), lax.axis_index("group")
     x = lax.rem(b, XS)
     plane = b - x
@@ -57,8 +59,16 @@
         return at(plane + lax.rem(x + steps, XS))
 
     nxt, prv = lax.rem(b + XS, n_blk), lax.rem(b + n_blk - XS, n_blk)
-    final = at(jnp.where(x == 0, nxt, b), lax.rem(g + 1, n_group))
-    final_from = at(jnp.where(x == 0, prv, b), lax.rem(g + n_group - 1, n_group))
+    to_blk, from_blk = jnp.where(x == 0, nxt, b), jnp.where(x == 0, prv, b)
+    final = at(to_blk, lax.rem(g + 1, n_group))
+    final_from = at(from_blk, lax.rem(g + n_group - 1, n_group))
+    first, last = lax.rem(g, YC) == 0, lax.rem(g, YC) == YC - 1
+    across = at(b, lax.rem(g + YC, n_group))
+    beside = at(to_blk, lax.rem(g + YC + 1, n_group))
+    barrier = pltpu.get_barrier_semaphore()
+
+    def greet(device):
+        pl.semaphore_signal(barrier, inc=1, device_id=device, device_id_type=MESH)
 
     loads = [
         pltpu.make_async_copy(u_in, users, load.at[0]),
@@ -69,9 +79,24 @@
     ]
     for copy in loads:
         copy.start()
-    barrier = pltpu.get_barrier_semaphore()
-    for device in (ring(1), ring(2), ring(3), at(nxt), at(prv), final, final_from):
-        pl.semaphore_signal(barrier, inc=1, device_id=device, device_id_type=MESH)
+    for device in (ring(1), ring(2), ring(3)):
+        greet(device)
+
+    @pl.when(x != 0)
+    def _():
+        greet(at(prv))
+
+    @pl.when(jnp.logical_not(first))
+    def _():
+        greet(final_from)
+
+    @pl.when(first | last)
+    def _():
+        greet(across)
+
+    @pl.when(first)
+    def _():
+        greet(at(from_blk, lax.rem(g + n_group - YC - 1, n_group)))
 
     def rows(k):
         return pl.ds(k * CH, CH)
@@ -100,6 +125,18 @@
         return pltpu.make_async_remote_copy(
             ref.at[slot(3), rows(k)], out.at[rows(k)], fsend.at[which, k], frecv.at[which, k],
             device_id=final, device_id_type=MESH)
+
+    def first_leg(which, k):
+        ref = (home_v, home_b)[which]
+        return pltpu.make_async_remote_copy(
+            ref.at[slot(3), rows(k)], relay.at[which, rows(k % HALF)], fsend.at[which, k], lrecv.at[which, k % HALF],
+            device_id=across if k < HALF else beside, device_id_type=MESH)
+
+    def second_leg(which, k):
+        out = (v_out, b_out)[which]
+        return pltpu.make_async_remote_copy(
+            relay.at[which, rows(k % HALF)], out.at[rows(k)], lsend.at[which, k % HALF], frecv.at[which, k],
+            device_id=beside if k < HALF else across, device_id_type=MESH)
 
     def send_v(s, k):
         @pl.when(x == XS - s)
@@ -131,7 +168,7 @@
     grad = 2.0 * dot3(gap, usplit, TN) + (2.0 * ridge_weight) * home_v[0]
     loads[3].wait()
     home_v[0], home_b[0] = adagrad(home_v[0], home_b[0], grad)
-    pl.semaphore_wait(barrier, 7)
+    pl.semaphore_wait(barrier, 4 + (x != 0).astype(jnp.int32) + (first | last).astype(jnp.int32))
     for k in range(NC):
         send_v(1, k)
     send_b(1)
@@ -173,8 +210,15 @@
             if s < STRATA - 1:
                 send_v(s + 1, k)
             else:
-                f_copy(0, k).start()
-                f_copy(1, k).start()
+                @pl.when(last)
+                def _():
+                    first_leg(0, k).start()
+                    first_leg(1, k).start()
+
+                @pl.when(jnp.logical_not(last))
+                def _():
+                    f_copy(0, k).start()
+                    f_copy(1, k).start()
         if s < STRATA - 1:
             send_b(s + 1)
 
@@ -187,6 +231,17 @@
         for which in range(2):
             for k in range(NC):
                 m_copy(which, k).wait_send()
+
+    for role, chunks in ((last, range(HALF)), (first, range(HALF, NC))):
+        @pl.when(role)
+        def _():
+            for k in chunks:
+                for which in range(2):
+                    first_leg(which, k).wait_recv()
+                    second_leg(which, k).start()
+            for k in chunks:
+                for which in range(2):
+                    second_leg(which, k).wait_send()
 
     for which in range(2):
         for k in range(NC):
@@ -213,11 +268,12 @@
             pltpu.VMEM((R, R), bf16), pltpu.VMEM((R, R), bf16),
             pltpu.VMEM((R, R), bf16), pltpu.VMEM((R, R), bf16),
             pltpu.VMEM((R, R), bf16), pltpu.VMEM((R, R), bf16),
+            pltpu.VMEM((2, R // 2, R), f32),
             dma((5,)), dma((2,)),
             dma((3, NC)), dma((3, NC)), dma((3, NC)), dma((3, NC)),
-            dma((2, NC)), dma((2, NC)), dma((2, NC)), dma((2, NC)),
+            dma((2, NC)), dma((2, NC)), dma((2, NC)), dma((2, NC)), dma((2, HALF)), dma((2, HALF)),
         ],
-        compiler_params=pltpu.CompilerParams(collective_id=0, has_side_effects=True, vmem_limit_bytes=32 * 2**20),
+        compiler_params=pltpu.CompilerParams(collective_id=0, has_side_effects=True, vmem_limit_bytes=60 * 2**20),
         name="strata",
     )(user_factors, user_state, item_factors, item_state, counts)
 

time: 115 us -> 90.4 us (0.79)
  the two profiles are of different devices: /device:TPU:128 before, /device:TPU:320 now
where the time goes in v2:
time: 90.4 us; the launch traced here: 90.1 us
  Pallas kernels  85 us (94%)
  local copies, waits for them, and re-layouts  4.5 us (5%)
    pallas_call x1, Pallas kernels, body(): pl.pallas_call(functools.partial(kernel, lax.axis_size('blk'), lax.axis_s...  85 us
    unnamed x10, local copies, waits for them, and re-layouts  4.5 us

profile of v2, /device:TPU:320, one launch (start us, length us, event | category | flops | bytes accessed | tf_op | source)
XLA Modules:
  0.0 90.1 jit_solution(13393506712657924974)
XLA Ops:
  0.6 85.0 %strata.1 = (f32[256,256]{1,0:T(8,128)}, f32[256,256]{1,0:T(8,128)}, f32[256,256]{1,0:T(8,128)}, f32[256,256]{1,0:T(8,128)}) custom-call(f32[256,256]{1,0:T(8,128)} %u_in.1, f32[256,256]{1,0:T(8,128)} %a_in.1, f32[256,256]{1,0:T(8,128)} %v_in.1, f32[256,256]{1,0:T(8,128)} %b_in.1, s32[256,1024]{1,0:T(8,128)} %k_in.1), custom_call_target="tpu_custom_call" | custom-call | tf_op jit(solution)/shard_map/strata/pallas_call | solution.py:258
  85.6 0.0 copy-start.2
  85.6 1.7 %copy.13 = f32[256,256]{1,0:T(8,128)} copy(f32[256,256]{1,0:T(8,128)} %get-tuple-element.8) | data formatting | bytes 524288
  87.3 0.0 copy-done.2
  87.4 0.0 copy-start.1
  87.4 0.7 copy.14
  88.1 0.3 copy-done.1
  88.4 0.0 copy-start
  88.4 0.7 copy.15
  89.1 0.3 copy-done
  89.4 0.7 copy.16
Async XLA Ops:
  85.6 1.7 %copy-start.2 = (f32[256,256]{1,0:T(8,128)S(1)}, f32[256,256]{1,0:T(8,128)}, u32[]{:S(2)}) copy-start(f32[256,256]{1,0:T(8,128)} %get-tuple-element.9) | copy-start | bytes 786436
  87.4 1.0 %copy-start.1 = (f32[256,256]{1,0:T(8,128)S(1)}, f32[256,256]{1,0:T(8,128)}, u32[]{:S(2)}) copy-start(f32[256,256]{1,0:T(8,128)} %get-tuple-element.10) | copy-start | bytes 786436
  88.4 1.0 %copy-start = (f32[256,256]{1,0:T(8,128)S(1)}, f32[256,256]{1,0:T(8,128)}, u32[]{:S(2)}) copy-start(f32[256,256]{1,0:T(8,128)} %get-tuple-element.11) | copy-start | bytes 786436

commit v3 on v1

v3 whole, which is shorter than its diff:
```python
import functools
import jax
import jax.numpy as jnp
from jax import lax
from jax.experimental import pallas as pl
from jax.experimental.pallas import tpu as pltpu
from jax.sharding import PartitionSpec as P

STRATA = 4
R = 256
XS = 4
YC = 16
NC = 4
CH = R // NC
LANES = (1, 3, 5, 7, 9, 11, 13, 14)
NP = len(LANES)
PIECE = R // NP
MESH = pl.DeviceIdType.MESH

conf_scale = 0.5
ridge_weight = 0.01
step_rate = 0.1

NT = (((1,), (1,)), ((), ()))
NN = (((1,), (0,)), ((), ()))
TN = (((0,), (0,)), ((), ()))


def split(value):
    high = value.astype(jnp.bfloat16)
    return high, (value - high.astype(jnp.float32)).astype(jnp.bfloat16)


def dot3(left, right, dims):
    (lh, ll), (rh, rl) = left, right
    dot = functools.partial(lax.dot_general, dimension_numbers=dims, preferred_element_type=jnp.float32)
    return dot(lh, rh) + (dot(lh, rl) + dot(ll, rh))


def weigh(counts, predicted):
    prefer = (counts > 0).astype(jnp.float32)
    return (1.0 + conf_scale * counts) * (predicted - prefer)


def adagrad(value, acc, grad):
    acc = acc + grad * grad
    return value - step_rate * grad * lax.rsqrt(acc), acc


def kernel(n_blk, n_group, u_in, a_in, v_in, b_in, k_in, u_out, a_out, e_out, v_out, b_out, g_out,
           users, user_acc, user_grad, home_v, home_b, kraw, kt, vin, gin, gout, uh, ul, vh, vl, gh, gl, relay, far, far_grad,
           load, store, vsend, vrecv, gsend, grecv, msend, mrecv, fsend, frecv, asend, arecv, zsend, zrecv, far_store):
    b, g = lax.axis_index("blk"), lax.axis_index("group")
    x = lax.rem(b, XS)
    plane = b - x

    def at(blk, group=g):
        return {"blk": blk, "group": group}

    def moved(blk_steps, group_steps=0):
        return at(lax.rem(b + blk_steps + n_blk, n_blk), lax.rem(g + group_steps + n_group, n_group))

    def ring(steps):
        return at(plane + lax.rem(x + steps, XS))

    def flag(condition):
        return condition.astype(jnp.int32)

    nxt, prv = moved(XS), moved(-XS)
    gone = jnp.where(x <= 1, XS, 0)
    lane = lax.rem(g, YC)
    first, last = lane == 0, lane == YC - 1
    relays = [lane == other for other in LANES]
    relaying = functools.reduce(jnp.logical_or, relays)

    loads = [
        pltpu.make_async_copy(u_in, users, load.at[0]),
        pltpu.make_async_copy(v_in, home_v.at[0], load.at[1]),
        pltpu.make_async_copy(k_in, kraw, load.at[2]),
        pltpu.make_async_copy(b_in, home_b.at[0], load.at[3]),
        pltpu.make_async_copy(a_in, user_acc, load.at[4]),
    ]
    for copy in loads:
        copy.start()

    barrier = pltpu.get_barrier_semaphore()

    def greet(*devices):
        for device in devices:
            pl.semaphore_signal(barrier, inc=1, device_id=device, device_id_type=MESH)

    greet(ring(1), ring(2), ring(3))

    @pl.when(x == 0)
    def _():
        greet(moved(1 - XS), moved(2 - XS), moved(3 - XS))

    @pl.when(x >= 2)
    def _():
        greet(prv)

    @pl.when(jnp.logical_not(first))
    def _():
        greet(moved(-gone, -1), moved(-1, -1))

    @pl.when(first)
    def _():
        greet(*[moved(-gone, other - YC) for other in LANES])

    @pl.when(first & (x == 1))
    def _():
        greet(*[moved(0, other - YC) for other in LANES])

    @pl.when(relaying)
    def _():
        greet(at(b, g - lane + YC - 1), at(plane + lax.rem(x + XS - 1, XS), g - lane + YC - 1))

    def rows(k):
        return pl.ds(k * CH, CH)

    def slot(s):
        return flag(x >= XS - s)

    def remote(src, dst, send, recv, device):
        return pltpu.make_async_remote_copy(src, dst, send, recv, device_id=device, device_id_type=MESH)

    def v_copy(s, k, device=None):
        return remote(home_v.at[slot(s - 1), rows(k)], vin.at[s - 1, rows(k)], vsend.at[s - 1, k], vrecv.at[s - 1, k],
                      ring(s) if device is None else device)

    def g_copy(s, k):
        return remote(gout.at[s - 1, rows(k)], gin.at[s - 1, rows(k)], gsend.at[s - 1, k], grecv.at[s - 1, k], ring(XS - s))

    def m_copy(which, k):
        ref = (home_v, home_b)[which]
        return remote(ref.at[0, rows(k)], ref.at[1, rows(k)], msend.at[which, k], mrecv.at[which, k], nxt)

    def home_rows(which, k):
        return (home_v, home_b)[which].at[slot(2), rows(k)]

    def steps(which):
        return 1 if which >= 2 else gone

    def f_copy(which, k):
        src = gout.at[2, rows(k)] if which == 2 else home_rows(which, k)
        return remote(src, (v_out, b_out, g_out)[which].at[rows(k)], fsend.at[which, k], frecv.at[which, k],
                      moved(steps(which), 1))

    def part(p):
        return pl.ds(p * PIECE, PIECE)

    def first_leg(which, p):
        src = ((home_v, home_b)[which].at[slot(2), part(p)] if which < 2 else
               users.at[part(p)] if which == 2 else kt.at[2, part(p)])
        return remote(src, relay.at[which], zsend.at[which, p], arecv.at[which], at(b if which < 2 else plane + lax.rem(x + 1, XS), g + LANES[p] - YC + 1))

    def last_leg(which, p):
        return remote(relay.at[which], far.at[which, part(p)], asend.at[which], zrecv.at[which, p],
                      moved(gone if which < 2 else jnp.where(x == 0, XS, 0), YC - LANES[p]))

    def send_far(which):
        for p in range(NP):
            first_leg(which, p).start()

    def pass_on(arrays):
        for role, p in zip(relays, range(NP)):
            @pl.when(role)
            def _():
                for which in arrays:
                    first_leg(which, p).wait_recv()
                    last_leg(which, p).start()

    def send_v(s, k):
        @pl.when(x == XS - s)
        def _():
            v_copy(s, k, moved(s)).start()

        @pl.when(x != XS - s)
        def _():
            v_copy(s, k).start()

    def migrate(s):
        @pl.when(x == XS - s)
        def _():
            for k in range(NC):
                m_copy(0, k).start()
                m_copy(1, k).start()

    def user_gradient(grad):
        return 2.0 * grad + (2.0 * ridge_weight) * users[...]

    def update_users(grad):
        users[...], user_acc[...] = adagrad(users[...], user_acc[...], user_gradient(grad))
        uh[...], ul[...] = split(users[...])

    loads[0].wait()
    uh[...], ul[...] = split(users[...])
    loads[1].wait()
    vh[...], vl[...] = split(home_v[0])
    loads[2].wait()
    usplit, vsplit = (uh[...], ul[...]), (vh[...], vl[...])
    gap = split(weigh(kraw[:, :R].astype(jnp.float32), dot3(usplit, vsplit, NT)))
    grad = 2.0 * dot3(gap, usplit, TN) + (2.0 * ridge_weight) * home_v[0]
    loads[3].wait()
    home_v[0], home_b[0] = adagrad(home_v[0], home_b[0], grad)
    pl.semaphore_wait(barrier, 3 + flag(x != 0) + flag(x >= 2) + jnp.where(last, 2 * NP, 2) + flag(relaying) + flag(relaying & (x == 1)))
    for k in range(NC):
        send_v(1, k)
    migrate(1)
    loads[4].wait()
    update_users(dot3(gap, vsplit, NN))
    for s in range(STRATA - 1, 0, -1):
        kt[s - 1] = kraw[:, s * R : (s + 1) * R].astype(jnp.float32).T
        if s == STRATA - 1:
            @pl.when(last)
            def _():
                send_far(3)

    for s in range(1, STRATA):
        ends = s == STRATA - 1
        for k in range(NC):
            v_copy(s, k).wait_recv()
            items = vin[s - 1, rows(k)]
            items_split = split(items)
            vh[rows(k)], vl[rows(k)] = items_split
            usplit = (uh[...], ul[...])
            gap = split(weigh(kt[s - 1, rows(k)], dot3(items_split, usplit, NT)))
            gh[rows(k)], gl[rows(k)] = gap
            gout[s - 1, rows(k)] = 2.0 * dot3(gap, usplit, NN) + (2.0 * ridge_weight) * items
            if ends:
                @pl.when(jnp.logical_not(last))
                def _():
                    f_copy(2, k).start()

                if k < 2:
                    pass_on(((2,), (0, 1))[k])
            else:
                g_copy(s, k).start()
        grad = dot3((gh[...], gl[...]), (vh[...], vl[...]), TN)
        if ends:
            user_grad[...] = user_gradient(grad)
            break
        update_users(grad)
        if s == STRATA - 2:
            stores = [pltpu.make_async_copy(users, u_out, store.at[0]), pltpu.make_async_copy(user_acc, a_out, store.at[1])]
            for copy in stores:
                copy.start()

            @pl.when(last)
            def _():
                send_far(2)
        for k in range(NC):
            @pl.when(x == XS - s)
            def _():
                m_copy(0, k).wait_recv()
                m_copy(1, k).wait_recv()

            @pl.when(x != XS - s)
            def _():
                v_copy(s, k).wait_send()

            g_copy(s, k).wait_recv()
            now = slot(s)
            home_v[now, rows(k)], home_b[now, rows(k)] = adagrad(home_v[now, rows(k)], home_b[now, rows(k)], gin[s - 1, rows(k)])
            send_v(s + 1, k)
        if s == STRATA - 2:
            @pl.when(last)
            def _():
                send_far(0)
                send_far(1)

            @pl.when(jnp.logical_not(last))
            def _():
                for k in range(NC):
                    f_copy(0, k).start()
                    f_copy(1, k).start()
        else:
            migrate(s + 1)
            pass_on((3,))
    stores.append(pltpu.make_async_copy(user_grad, e_out, store.at[2]))
    stores[2].start()

    @pl.when(first)
    def _():
        for p in range(NP):
            for which in range(4):
                last_leg(which, p).wait_recv()
        copies = [pltpu.make_async_copy(far.at[0], v_out, far_store.at[0]), pltpu.make_async_copy(far.at[1], b_out, far_store.at[1])]
        for copy in copies:
            copy.start()
        items, usplit = far[0], split(far[2])
        gap = split(weigh(far[3], dot3(split(items), usplit, NT)))
        far_grad[...] = 2.0 * dot3(gap, usplit, NN) + (2.0 * ridge_weight) * items
        copies.append(pltpu.make_async_copy(far_grad, g_out, far_store.at[2]))
        copies[2].start()
        for copy in copies:
            copy.wait()

    for which in range(4):
        @pl.when(relaying)
        def _():
            last_leg(which, 0).wait_send()

        @pl.when(last)
        def _():
            for p in range(NP):
                first_leg(which, p).wait_send()

    for s in range(1, STRATA):
        for k in range(NC):
            if s < STRATA - 1:
                g_copy(s, k).wait_send()

                @pl.when(x == XS - s)
                def _():
                    v_copy(s, k).wait_send()
            else:
                v_copy(s, k).wait_send()

    @pl.when(x >= 2)
    def _():
        for which in range(2):
            for k in range(NC):
                m_copy(which, k).wait_send()

    for which in range(3):
        for k in range(NC):
            @pl.when(jnp.logical_not(last))
            def _():
                f_copy(which, k).wait_send()

            @pl.when(jnp.logical_not(first))
            def _():
                f_copy(which, k).wait_recv()
    for copy in stores:
        copy.wait()


def last_step(value, acc, grad):
    acc = acc + grad * grad
    return value - step_rate * grad / jnp.sqrt(acc), acc


def body(user_factors, user_state, item_factors, item_state, counts):
    anywhere = pl.BlockSpec(memory_space=pl.ANY)
    block = jax.ShapeDtypeStruct((R, R), jnp.float32)
    f32, bf16 = jnp.float32, jnp.bfloat16
    dma = pltpu.SemaphoreType.DMA
    users, user_acc, user_grad, items, item_acc, item_grad = pl.pallas_call(
        functools.partial(kernel, lax.axis_size("blk"), lax.axis_size("group")),
        out_shape=(block,) * 6,
        in_specs=[anywhere] * 5,
        out_specs=(anywhere,) * 6,
        scratch_shapes=[
            pltpu.VMEM((R, R), f32), pltpu.VMEM((R, R), f32), pltpu.VMEM((R, R), f32),
            pltpu.VMEM((2, R, R), f32), pltpu.VMEM((2, R, R), f32),
            pltpu.VMEM((R, STRATA * R), jnp.int32), pltpu.VMEM((3, R, R), f32),
            pltpu.VMEM((3, R, R), f32), pltpu.VMEM((2, R, R), f32), pltpu.VMEM((3, R, R), f32),
            pltpu.VMEM((R, R), bf16), pltpu.VMEM((R, R), bf16),
            pltpu.VMEM((R, R), bf16), pltpu.VMEM((R, R), bf16),
            pltpu.VMEM((R, R), bf16), pltpu.VMEM((R, R), bf16),
            pltpu.VMEM((4, PIECE, R), f32), pltpu.VMEM((4, R, R), f32), pltpu.VMEM((R, R), f32),
            dma((5,)), dma((3,)),
            dma((3, NC)), dma((3, NC)), dma((2, NC)), dma((2, NC)),
            dma((2, NC)), dma((2, NC)), dma((3, NC)), dma((3, NC)), dma((4,)), dma((4,)), dma((4, NP)), dma((4, NP)), dma((3,)),
        ],
        compiler_params=pltpu.CompilerParams(collective_id=0, has_side_effects=True, vmem_limit_bytes=60 * 2**20),
        name="strata",
    )(user_factors, user_state, item_factors, item_state, counts)
    return last_step(users, user_acc, user_grad) + last_step(items, item_acc, item_grad)


def solution(mesh):
    spec = P(("blk", "group"), None)
    return jax.shard_map(body, mesh=mesh, in_specs=(spec,) * 5, out_specs=(spec,) * 4, check_vma=False)
```

time: 115 us -> 79.9 us (0.69)
  the two profiles are of different devices: /device:TPU:128 before, /device:TPU:2 now
where the time goes in v3:
time: 79.9 us; the launch traced here: 79.7 us
  Pallas kernels  76.7 us (96%)
  other arithmetic  2.36 us (3%)
    pallas_call x1, Pallas kernels, body(): pl.pallas_call(functools.partial(kernel, lax.axis_size('blk'), lax.axis_s...  76.7 us
    sub x1, other arithmetic, last_step(): return (value - step_rate * grad / jnp.sqrt(acc), acc)  2.36 us

profile of v3, /device:TPU:2, one launch (start us, length us, event | category | flops | bytes accessed | tf_op | source)
XLA Modules:
  0.0 79.7 jit_solution(9775227371414816240)
XLA Ops:
  0.6 76.7 %strata.1 = (f32[256,256]{1,0:T(8,128)}, f32[256,256]{1,0:T(8,128)}, f32[256,256]{1,0:T(8,128)}, f32[256,256]{1,0:T(8,128)}, f32[256,256]{1,0:T(8,128)}, /*index=5*/f32[256,256]{1,0:T(8,128)}) custom-call(f32[256,256]{1,0:T(8,128)} %u_in.1, f32[256,256]{1,0:T(8,128)} %a_in.1, f32[256,256]{1,0:T(8,128)} %v_in.1, f32[256,256]{1,0:T(8,128)} %b_in.1, ...), custom_call_target="tpu_custom_call" | custom-call | tf_op jit(solution)/shard_map/strata/pallas_call | solution.py:349
  77.3 2.4 %multiply_subtract_fusion = (f32[256,256]{1,0:T(8,128)}, f32[256,256]{1,0:T(8,128)}, f32[256,256]{1,0:T(8,128)}, f32[256,256]{1,0:T(8,128)}) fusion(f32[256,256]{1,0:T(8,128)} %get-tuple-element.13, f32[256,256]{1,0:T(8,128)} %get-tuple-element.14, f32[256,256]{1,0:T(8,128)} %get-tuple-element.15, f32[256,256]{1,0:T(8,128)} %get-tuple-element.10, ...), kind=kLoop, calls=%fused_computation | loop fusion | flops 655360 | bytes 2621440 | tf_op jit(solution)/shard_map/sub | solution.py:341

commit v4 on v3

--- a/solution.py
+++ b/solution.py
@@ -49,10 +49,11 @@
 
 def kernel(n_blk, n_group, u_in, a_in, v_in, b_in, k_in, u_out, a_out, e_out, v_out, b_out, g_out,
            users, user_acc, user_grad, home_v, home_b, kraw, kt, vin, gin, gout, uh, ul, vh, vl, gh, gl, relay, far, far_grad,
-           load, store, vsend, vrecv, gsend, grecv, msend, mrecv, fsend, frecv, asend, arecv, zsend, zrecv, far_store):
+           load, store, vsend, vrecv, gsend, grecv, msend, mrecv, fsend, frecv, asend, arecv, zsend, zrecv, far_store, hsend):
     b, g = lax.axis_index("blk"), lax.axis_index("group")
     x = lax.rem(b, XS)
     plane = b - x
+    low, high = b < XS, b >= n_blk - XS
 
     def at(blk, group=g):
         return {"blk": blk, "group": group}
@@ -107,13 +108,15 @@
     def _():
         greet(*[moved(-gone, other - YC) for other in LANES])
 
-    @pl.when(first & (x == 1))
-    def _():
-        greet(*[moved(0, other - YC) for other in LANES])
+    @pl.when(first & (x == 1) & low)
+    def _():
+        greet(*[moved(-gone, other) for other in LANES])
+
+    far_user = YC - 1 - lane + jnp.where((x == 1) & high, YC, 0)
 
     @pl.when(relaying)
     def _():
-        greet(at(b, g - lane + YC - 1), at(plane + lax.rem(x + XS - 1, XS), g - lane + YC - 1))
+        greet(moved(0, YC - 1 - lane), moved(gone - 1, far_user))
 
     def rows(k):
         return pl.ds(k * CH, CH)
@@ -149,14 +152,19 @@
     def part(p):
         return pl.ds(p * PIECE, PIECE)
 
+    def hand_on(k):
+        return remote(vin.at[2, rows(k)], v_out.at[rows(k)], hsend.at[k], frecv.at[0, k], moved(1, 1))
+
     def first_leg(which, p):
         src = ((home_v, home_b)[which].at[slot(2), part(p)] if which < 2 else
                users.at[part(p)] if which == 2 else kt.at[2, part(p)])
-        return remote(src, relay.at[which], zsend.at[which, p], arecv.at[which], at(b if which < 2 else plane + lax.rem(x + 1, XS), g + LANES[p] - YC + 1))
+        there = (moved(0, LANES[p] - YC + 1) if which < 2 else
+                 moved(jnp.where((x == 0) | (x == XS - 1), 1 - XS, 1), LANES[p] - YC + 1 + jnp.where((x == 0) & low, YC, 0)))
+        return remote(src, relay.at[which], zsend.at[which, p], arecv.at[which], there)
 
     def last_leg(which, p):
         return remote(relay.at[which], far.at[which, part(p)], asend.at[which], zrecv.at[which, p],
-                      moved(gone if which < 2 else jnp.where(x == 0, XS, 0), YC - LANES[p]))
+                      moved(gone, YC - LANES[p] - (0 if which < 2 else jnp.where((x == 1) & high, YC, 0))))
 
     def send_far(which):
         for p in range(NP):
@@ -196,19 +204,26 @@
     loads[0].wait()
     uh[...], ul[...] = split(users[...])
     loads[1].wait()
-    vh[...], vl[...] = split(home_v[0])
-    loads[2].wait()
-    usplit, vsplit = (uh[...], ul[...]), (vh[...], vl[...])
-    gap = split(weigh(kraw[:, :R].astype(jnp.float32), dot3(usplit, vsplit, NT)))
-    grad = 2.0 * dot3(gap, usplit, TN) + (2.0 * ridge_weight) * home_v[0]
-    loads[3].wait()
-    home_v[0], home_b[0] = adagrad(home_v[0], home_b[0], grad)
-    pl.semaphore_wait(barrier, 3 + flag(x != 0) + flag(x >= 2) + jnp.where(last, 2 * NP, 2) + flag(relaying) + flag(relaying & (x == 1)))
-    for k in range(NC):
-        send_v(1, k)
+    usplit, grad = (uh[...], ul[...]), 0.0
+    for h in range(2):
+        half = pl.ds(h * R // 2, R // 2)
+        items = home_v[0, half]
+        items_split = split(items)
+        if h == 0:
+            loads[2].wait()
+        gap = split(weigh(kraw[:, half].astype(jnp.float32), dot3(usplit, items_split, NT)))
+        item_grad = 2.0 * dot3(gap, usplit, TN) + (2.0 * ridge_weight) * items
+        if h == 0:
+            loads[3].wait()
+        home_v[0, half], home_b[0, half] = adagrad(items, home_b[0, half], item_grad)
+        if h == 0:
+            pl.semaphore_wait(barrier, 3 + flag(x != 0) + flag(x >= 2) + jnp.where(last, 2 * NP, 2) + flag(relaying) + flag(relaying & (x == 1) & high))
+        for k in range(h * NC // 2, (h + 1) * NC // 2):
+            send_v(1, k)
+        grad = grad + dot3(gap, items_split, NN)
     migrate(1)
     loads[4].wait()
-    update_users(dot3(gap, vsplit, NN))
+    update_users(grad)
     for s in range(STRATA - 1, 0, -1):
         kt[s - 1] = kraw[:, s * R : (s + 1) * R].astype(jnp.float32).T
         if s == STRATA - 1:
@@ -220,6 +235,10 @@
         ends = s == STRATA - 1
         for k in range(NC):
             v_copy(s, k).wait_recv()
+            if ends:
+                @pl.when(jnp.logical_not(last) & (x == 0))
+                def _():
+                    hand_on(k).start()
             items = vin[s - 1, rows(k)]
             items_split = split(items)
             vh[rows(k)], vl[rows(k)] = items_split
@@ -232,8 +251,17 @@
                 def _():
                     f_copy(2, k).start()
 
-                if k < 2:
-                    pass_on(((2,), (0, 1))[k])
+                if k == 0:
+                    pass_on((0, 1))
+
+                    @pl.when(x == 1)
+                    def _():
+                        pass_on((2,))
+                if k == 2:
+                    @pl.when(jnp.logical_not(last) & (x == 0))
+                    def _():
+                        for w in range(2 * NC):
+                            f_copy(w // NC, w % NC).start()
             else:
                 g_copy(s, k).start()
         grad = dot3((gh[...], gl[...]), (vh[...], vl[...]), TN)
@@ -263,17 +291,26 @@
             now = slot(s)
             home_v[now, rows(k)], home_b[now, rows(k)] = adagrad(home_v[now, rows(k)], home_b[now, rows(k)], gin[s - 1, rows(k)])
             send_v(s + 1, k)
+            if s == STRATA - 2:
+                @pl.when(last)
+                def _():
+                    for p in range(k * NP // NC, (k + 1) * NP // NC):
+                        first_leg(0, p).start()
+                        first_leg(1, p).start()
         if s == STRATA - 2:
-            @pl.when(last)
-            def _():
-                send_far(0)
-                send_far(1)
-
-            @pl.when(jnp.logical_not(last))
+            @pl.when(jnp.logical_not(last) & (x == 1))
+            def _():
+                for k in range(NC):
+                    f_copy(1, k).start()
+
+            @pl.when(jnp.logical_not(last) & (x >= 2))
             def _():
                 for k in range(NC):
                     f_copy(0, k).start()
                     f_copy(1, k).start()
+            @pl.when(x != 1)
+            def _():
+                pass_on((2,))
         else:
             migrate(s + 1)
             pass_on((3,))
@@ -283,16 +320,20 @@
     @pl.when(first)
     def _():
         for p in range(NP):
-            for which in range(4):
+            last_leg(2, p).wait_recv()
+        usplit = split(far[2])
+        copies = []
+        for p in range(NP):
+            for which in (3, 0, 1):
                 last_leg(which, p).wait_recv()
-        copies = [pltpu.make_async_copy(far.at[0], v_out, far_store.at[0]), pltpu.make_async_copy(far.at[1], b_out, far_store.at[1])]
-        for copy in copies:
-            copy.start()
-        items, usplit = far[0], split(far[2])
-        gap = split(weigh(far[3], dot3(split(items), usplit, NT)))
-        far_grad[...] = 2.0 * dot3(gap, usplit, NN) + (2.0 * ridge_weight) * items
-        copies.append(pltpu.make_async_copy(far_grad, g_out, far_store.at[2]))
-        copies[2].start()
+            for which, out in ((0, v_out), (1, b_out)):
+                copies.append(pltpu.make_async_copy(far.at[which, part(p)], out.at[part(p)], far_store.at[which, p]))
+                copies[-1].start()
+            items = far[0, part(p)]
+            gap = split(weigh(far[3, part(p)], dot3(split(items), usplit, NT)))
+            far_grad[part(p)] = 2.0 * dot3(gap, usplit, NN) + (2.0 * ridge_weight) * items
+            copies.append(pltpu.make_async_copy(far_grad.at[part(p)], g_out.at[part(p)], far_store.at[2, p]))
+            copies[-1].start()
         for copy in copies:
             copy.wait()
 
@@ -325,13 +366,18 @@
 
     for which in range(3):
         for k in range(NC):
-            @pl.when(jnp.logical_not(last))
+            @pl.when(jnp.logical_not(last) & ((x != 1) | (which != 0)))
             def _():
                 f_copy(which, k).wait_send()
 
             @pl.when(jnp.logical_not(first))
             def _():
                 f_copy(which, k).wait_recv()
+    @pl.when(jnp.logical_not(last) & (x == 0))
+    def _():
+        for k in range(NC):
+            hand_on(k).wait_send()
+
     for copy in stores:
         copy.wait()
 
@@ -362,7 +408,7 @@
             pltpu.VMEM((4, PIECE, R), f32), pltpu.VMEM((4, R, R), f32), pltpu.VMEM((R, R), f32),
             dma((5,)), dma((3,)),
             dma((3, NC)), dma((3, NC)), dma((2, NC)), dma((2, NC)),
-            dma((2, NC)), dma((2, NC)), dma((3, NC)), dma((3, NC)), dma((4,)), dma((4,)), dma((4, NP)), dma((4, NP)), dma((3,)),
+            dma((2, NC)), dma((2, NC)), dma((3, NC)), dma((3, NC)), dma((4,)), dma((4,)), dma((4, NP)), dma((4, NP)), dma((3, NP)), dma((NC,)),
         ],
         compiler_params=pltpu.CompilerParams(collective_id=0, has_side_effects=True, vmem_limit_bytes=60 * 2**20),
         name="strata",

time: 79.9 us -> 76.1 us (0.952)
  the two profiles are of different devices: /device:TPU:2 before, /device:TPU:194 now
where the time goes in v4:
time: 76.1 us; the launch traced here: 75.9 us
  Pallas kernels  72.9 us (96%)
  other arithmetic  2.36 us (3%)
    pallas_call x1, Pallas kernels, body(): pl.pallas_call(functools.partial(kernel, lax.axis_size('blk'), lax.axis_s...  72.9 us
    sub x1, other arithmetic, last_step(): return (value - step_rate * grad / jnp.sqrt(acc), acc)  2.36 us

profile of v4, /device:TPU:194, one launch (start us, length us, event | category | flops | bytes accessed | tf_op | source)
XLA Modules:
  0.0 75.9 jit_solution(16332569387861122345)
XLA Ops:
  0.6 72.9 %strata.1 = (f32[256,256]{1,0:T(8,128)}, f32[256,256]{1,0:T(8,128)}, f32[256,256]{1,0:T(8,128)}, f32[256,256]{1,0:T(8,128)}, f32[256,256]{1,0:T(8,128)}, /*index=5*/f32[256,256]{1,0:T(8,128)}) custom-call(f32[256,256]{1,0:T(8,128)} %u_in.1, f32[256,256]{1,0:T(8,128)} %a_in.1, f32[256,256]{1,0:T(8,128)} %v_in.1, f32[256,256]{1,0:T(8,128)} %b_in.1, ...), custom_call_target="tpu_custom_call" | custom-call | tf_op jit(solution)/shard_map/strata/pallas_call | solution.py:395
  73.5 2.4 %multiply_subtract_fusion = (f32[256,256]{1,0:T(8,128)}, f32[256,256]{1,0:T(8,128)}, f32[256,256]{1,0:T(8,128)}, f32[256,256]{1,0:T(8,128)}) fusion(f32[256,256]{1,0:T(8,128)} %get-tuple-element.13, f32[256,256]{1,0:T(8,128)} %get-tuple-element.14, f32[256,256]{1,0:T(8,128)} %get-tuple-element.15, f32[256,256]{1,0:T(8,128)} %get-tuple-element.10, ...), kind=kLoop, calls=%fused_computation | loop fusion | flops 655360 | bytes 2621440 | tf_op jit(solution)/shard_map/sub | solution.py:387

commit v5 on v4

--- a/solution.py
+++ b/solution.py
@@ -151,6 +151,16 @@
 
     def part(p):
         return pl.ds(p * PIECE, PIECE)
+
+    later = jnp.logical_not(last) & (x <= 1) & (b < n_blk - XS)
+
+    def send_state():
+        for k in range(NC):
+            @pl.when(x != 1)
+            def _():
+                f_copy(0, k).start()
+
+            f_copy(1, k).start()
 
     def hand_on(k):
         return remote(vin.at[2, rows(k)], v_out.at[rows(k)], hsend.at[k], frecv.at[0, k], moved(1, 1))
@@ -258,10 +268,9 @@
                     def _():
                         pass_on((2,))
                 if k == 2:
-                    @pl.when(jnp.logical_not(last) & (x == 0))
+                    @pl.when(later)
                     def _():
-                        for w in range(2 * NC):
-                            f_copy(w // NC, w % NC).start()
+                        send_state()
             else:
                 g_copy(s, k).start()
         grad = dot3((gh[...], gl[...]), (vh[...], vl[...]), TN)
@@ -298,16 +307,9 @@
                         first_leg(0, p).start()
                         first_leg(1, p).start()
         if s == STRATA - 2:
-            @pl.when(jnp.logical_not(last) & (x == 1))
-            def _():
-                for k in range(NC):
-                    f_copy(1, k).start()
-
-            @pl.when(jnp.logical_not(last) & (x >= 2))
-            def _():
-                for k in range(NC):
-                    f_copy(0, k).start()
-                    f_copy(1, k).start()
+            @pl.when(jnp.logical_not(last | later))
+            def _():
+                send_state()
             @pl.when(x != 1)
             def _():
                 pass_on((2,))

time: 76.1 us -> 76 us (level)
  no operation moved by 1% of the time
where the time goes in v5:
time: 76 us; the launch traced here: 75.8 us
  Pallas kernels  72.8 us (96%)
  other arithmetic  2.36 us (3%)
    pallas_call x1, Pallas kernels, body(): pl.pallas_call(functools.partial(kernel, lax.axis_size('blk'), lax.axis_s...  72.8 us
    sub x1, other arithmetic, last_step(): return (value - step_rate * grad / jnp.sqrt(acc), acc)  2.36 us

profile of v5, /device:TPU:194, one launch (start us, length us, event | category | flops | bytes accessed | tf_op | source)
XLA Modules:
  0.0 75.8 jit_solution(17832059698861864824)
XLA Ops:
  0.6 72.8 %strata.1 = (f32[256,256]{1,0:T(8,128)}, f32[256,256]{1,0:T(8,128)}, f32[256,256]{1,0:T(8,128)}, f32[256,256]{1,0:T(8,128)}, f32[256,256]{1,0:T(8,128)}, /*index=5*/f32[256,256]{1,0:T(8,128)}) custom-call(f32[256,256]{1,0:T(8,128)} %u_in.1, f32[256,256]{1,0:T(8,128)} %a_in.1, f32[256,256]{1,0:T(8,128)} %v_in.1, f32[256,256]{1,0:T(8,128)} %b_in.1, ...), custom_call_target="tpu_custom_call" | custom-call | tf_op jit(solution)/shard_map/strata/pallas_call | solution.py:397
  73.5 2.4 %multiply_subtract_fusion = (f32[256,256]{1,0:T(8,128)}, f32[256,256]{1,0:T(8,128)}, f32[256,256]{1,0:T(8,128)}, f32[256,256]{1,0:T(8,128)}) fusion(f32[256,256]{1,0:T(8,128)} %get-tuple-element.13, f32[256,256]{1,0:T(8,128)} %get-tuple-element.14, f32[256,256]{1,0:T(8,128)} %get-tuple-element.15, f32[256,256]{1,0:T(8,128)} %get-tuple-element.10, ...), kind=kLoop, calls=%fused_computation | loop fusion | flops 655360 | bytes 2621440 | tf_op jit(solution)/shard_map/sub | solution.py:389

commit v6 on v5

--- a/solution.py
+++ b/solution.py
@@ -77,9 +77,10 @@
     loads = [
         pltpu.make_async_copy(u_in, users, load.at[0]),
         pltpu.make_async_copy(v_in, home_v.at[0], load.at[1]),
-        pltpu.make_async_copy(k_in, kraw, load.at[2]),
+        pltpu.make_async_copy(k_in.at[:, pl.ds(0, R)], kraw.at[:, pl.ds(0, R)], load.at[2]),
         pltpu.make_async_copy(b_in, home_b.at[0], load.at[3]),
         pltpu.make_async_copy(a_in, user_acc, load.at[4]),
+        pltpu.make_async_copy(k_in.at[:, pl.ds(R, 3 * R)], kraw.at[:, pl.ds(R, 3 * R)], load.at[5]),
     ]
     for copy in loads:
         copy.start()
@@ -234,6 +235,7 @@
     migrate(1)
     loads[4].wait()
     update_users(grad)
+    loads[5].wait()
     for s in range(STRATA - 1, 0, -1):
         kt[s - 1] = kraw[:, s * R : (s + 1) * R].astype(jnp.float32).T
         if s == STRATA - 1:
@@ -408,7 +410,7 @@
             pltpu.VMEM((R, R), bf16), pltpu.VMEM((R, R), bf16),
             pltpu.VMEM((R, R), bf16), pltpu.VMEM((R, R), bf16),
             pltpu.VMEM((4, PIECE, R), f32), pltpu.VMEM((4, R, R), f32), pltpu.VMEM((R, R), f32),
-            dma((5,)), dma((3,)),
+            dma((6,)), dma((3,)),
             dma((3, NC)), dma((3, NC)), dma((2, NC)), dma((2, NC)),
             dma((2, NC)), dma((2, NC)), dma((3, NC)), dma((3, NC)), dma((4,)), dma((4,)), dma((4, NP)), dma((4, NP)), dma((3, NP)), dma((NC,)),
         ],

time: 76 us -> 75.9 us (level)
  no operation moved by 1% of the time
where the time goes in v6:
time: 75.9 us; the launch traced here: 75.7 us
  Pallas kernels  72.7 us (96%)
  other arithmetic  2.36 us (3%)
    pallas_call x1, Pallas kernels, body(): pl.pallas_call(functools.partial(kernel, lax.axis_size('blk'), lax.axis_s...  72.7 us
    sub x1, other arithmetic, last_step(): return (value - step_rate * grad / jnp.sqrt(acc), acc)  2.36 us

profile of v6, /device:TPU:194, one launch (start us, length us, event | category | flops | bytes accessed | tf_op | source)
XLA Modules:
  0.0 75.7 jit_solution(10559952075989527961)
XLA Ops:
  0.6 72.7 %strata.1 = (f32[256,256]{1,0:T(8,128)}, f32[256,256]{1,0:T(8,128)}, f32[256,256]{1,0:T(8,128)}, f32[256,256]{1,0:T(8,128)}, f32[256,256]{1,0:T(8,128)}, /*index=5*/f32[256,256]{1,0:T(8,128)}) custom-call(f32[256,256]{1,0:T(8,128)} %u_in.1, f32[256,256]{1,0:T(8,128)} %a_in.1, f32[256,256]{1,0:T(8,128)} %v_in.1, f32[256,256]{1,0:T(8,128)} %b_in.1, ...), custom_call_target="tpu_custom_call" | custom-call | tf_op jit(solution)/shard_map/strata/pallas_call | solution.py:399
  73.4 2.4 %multiply_subtract_fusion = (f32[256,256]{1,0:T(8,128)}, f32[256,256]{1,0:T(8,128)}, f32[256,256]{1,0:T(8,128)}, f32[256,256]{1,0:T(8,128)}) fusion(f32[256,256]{1,0:T(8,128)} %get-tuple-element.13, f32[256,256]{1,0:T(8,128)} %get-tuple-element.14, f32[256,256]{1,0:T(8,128)} %get-tuple-element.15, f32[256,256]{1,0:T(8,128)} %get-tuple-element.10, ...), kind=kLoop, calls=%fused_computation | loop fusion | flops 655360 | bytes 2621440 | tf_op jit(solution)/shard_map/sub | solution.py:391
